TPU v7x, 32 devices: a whole 2x2x4 slice. The times are simulated.
32 devices in a mesh: node: 8 (over z, y), local: 4 (over x, core).
Axes of the slice: x: 2, y: 2, z: 4, core: 2. Of those that a mesh axis runs over, the one named last changes fastest.
Arguments:
- tokens: bfloat16 [2048, 3584], P(('node', 'local')), may hold values from -6 to 6
- expert_ids: int32 [2048, 8], P(('node', 'local')), may hold values from 0 to 15, all different within a row; in each aligned block of 64 rows (0 to 63, 64 to 127, ...) at most 48 rows name the same one
- gate_values: float32 [2048, 8], P(('node', 'local')), may hold values from 0.1 to 1
- holder: int32 [16], replicated, may hold values from 0 to 15, each once
- matching: int32 [8], replicated, may hold values from 0 to 7, as said below
- gate_weight: bfloat16 [32, 3584, 512], P(('node', 'local')), may hold values from -0.09375 to 0.09375
- up_weight: bfloat16 [32, 3584, 512], P(('node', 'local')), may hold values from -0.09375 to 0.09375
- down_weight: bfloat16 [32, 512, 3584], P(('node', 'local')), may hold values from -0.1875 to 0.1875
Outputs:
- moe_out: bfloat16 [2048, 3584], P(('node', 'local'))
- new_gate: bfloat16 [32, 3584, 512], P(('node', 'local'))
- new_up: bfloat16 [32, 3584, 512], P(('node', 'local'))
- new_down: bfloat16 [32, 512, 3584], P(('node', 'local'))
Inputs may be any that keep to these rules, and one draw needn't show every extreme that they name: `expert_ids`: each row names 8 different experts. In the 64 rows of one device no expert is named more than 48 times, and some device names some expert exactly 48 times. `holder`: each expert appears once. A perfect matching of the nodes: matching[matching[n]] == n and matching[n] != n.
All inputs are finite; a program needn't handle non-finite values.
Results may differ from a plain program's by a relative error of at most 0.0065.
Values may be sent and summed in bfloat16 or wider, within the bound.
A program may use at most 192 MiB of HBM per device.

v0:
```python
import jax
import jax.numpy as jnp
from jax import lax
from jax.sharding import PartitionSpec as P


def expert_half(row_block, weights):
    gate_part, up_part, down_part = weights
    gate_proj = jnp.dot(row_block, gate_part[0], preferred_element_type=jnp.float32)
    up_proj = jnp.dot(row_block, up_part[0], preferred_element_type=jnp.float32)
    hidden = (jax.nn.silu(gate_proj) * up_proj).astype(jnp.bfloat16)
    return jnp.dot(hidden, down_part[0], preferred_element_type=jnp.float32).astype(jnp.bfloat16)


def split_parts(matrix, pieces):
    return matrix.reshape((pieces, matrix.shape[1] // pieces, matrix.shape[2]))


def move_weights(weights, matching):
    node_count = lax.axis_size("node")
    gate_part, up_part, down_part = weights
    arrived = (
        lax.all_to_all(
            split_parts(gate_part, node_count), "node", split_axis=0, concat_axis=0, tiled=True
        ),
        lax.all_to_all(
            split_parts(up_part, node_count), "node", split_axis=0, concat_axis=0, tiled=True
        ),
        lax.all_to_all(
            split_parts(down_part, node_count), "node", split_axis=0, concat_axis=0, tiled=True
        ),
    )
    reordered = tuple((jnp.take(block, matching, axis=0) for block in arrived))
    returned = (
        lax.all_to_all(reordered[0], "node", split_axis=0, concat_axis=0, tiled=True),
        lax.all_to_all(reordered[1], "node", split_axis=0, concat_axis=0, tiled=True),
        lax.all_to_all(reordered[2], "node", split_axis=0, concat_axis=0, tiled=True),
    )
    return (
        returned[0].reshape(gate_part.shape),
        returned[1].reshape(up_part.shape),
        returned[2].reshape(down_part.shape),
    )


def per_device(
    tokens, expert_ids, gate_values, holder, matching, gate_weight, up_weight, down_weight
):
    experts = holder.shape[0]
    tok_count, top_count = expert_ids.shape
    capacity = max(2, tok_count * top_count * 3 // (2 * experts))
    feature_count = tokens.shape[1]
    weights = (gate_weight, up_weight, down_weight)
    swapped = move_weights(weights, matching)
    expert_range = jnp.arange(experts, dtype=jnp.int32)
    old_slot = jnp.sum(
        jnp.where(holder[None, :] == expert_range[:, None], expert_range[None, :], 0), axis=1
    )
    flat_expert = expert_ids.reshape(-1)
    route_count = flat_expert.shape[0]
    one_hot = (flat_expert[:, None] == expert_range[None, :]).astype(jnp.int32)
    earlier = jnp.cumsum(one_hot, axis=0) - one_hot
    position = jnp.sum(earlier * one_hot, axis=1)
    destination = jnp.sum(one_hot * old_slot[None, :], axis=1)
    buffer_index = destination * capacity + position
    route_table = (
        jnp.full((experts * capacity,), route_count, jnp.int32)
        .at[buffer_index]
        .set(jnp.arange(route_count, dtype=jnp.int32))
    )
    padded_tokens = jnp.concatenate([tokens, jnp.zeros((1, feature_count), jnp.bfloat16)], axis=0)
    outgoing = padded_tokens[route_table // top_count]
    doubled = jnp.broadcast_to(
        outgoing.reshape(experts, 1, capacity, feature_count), (experts, 2, capacity, feature_count)
    ).reshape(2 * experts, capacity, feature_count)
    arrived = lax.all_to_all(doubled, ("node", "local"), split_axis=0, concat_axis=0, tiled=True)
    partial_value = expert_half(arrived.reshape(-1, feature_count), weights).reshape(arrived.shape)
    returned = lax.all_to_all(
        partial_value, ("node", "local"), split_axis=0, concat_axis=0, tiled=True
    )
    halves = returned.reshape(experts, 2, capacity, feature_count)
    summed = (
        (halves[:, 0].astype(jnp.float32) + halves[:, 1].astype(jnp.float32))
        .astype(jnp.bfloat16)
        .reshape(experts * capacity, feature_count)
    )
    picked = summed[buffer_index].astype(jnp.float32).reshape(tok_count, top_count, feature_count)
    combined = jnp.sum(picked * gate_values[:, :, None], axis=1).astype(jnp.bfloat16)
    return (combined, swapped[0], swapped[1], swapped[2])


def solution(mesh):
    in_specs = (
        P(("node", "local"), None),
        P(("node", "local"), None),
        P(("node", "local"), None),
        P(),
        P(),
        P(("node", "local"), None, None),
        P(("node", "local"), None, None),
        P(("node", "local"), None, None),
    )
    out_specs = (
        P(("node", "local"), None),
        P(("node", "local"), None, None),
        P(("node", "local"), None, None),
        P(("node", "local"), None, None),
    )
    return jax.shard_map(
        per_device, mesh=mesh, in_specs=in_specs, out_specs=out_specs, check_vma=False
    )
```

profile of v0, /device:TPU:0, one launch (start us, length us, event | category | flops | bytes accessed | tf_op | source)
XLA Modules:
  0.0 1058.2 jit_solution(665721320491443558)
XLA Ops:
  0.6 0.0 copy-start.1
  0.6 89.6 %all_to_all.40 = bf16[8,448,512]{2,1,0:T(8,128)(2,1)} all-to-all(bf16[8,448,512]{2,1,0:T(8,128)(2,1)} %bitcast.66), channel_id=1, replica_groups=mesh['node'=8,'local'=4] {'node'}, dimensions={0} | all-to-all | bytes 7340032 | tf_op jit(solution)/shard_map/all_to_all | solution.py:23
  90.2 0.0 copy-done.1
  90.2 85.3 %all_to_all.41 = bf16[8,448,512]{2,1,0:T(8,128)(2,1)} all-to-all(bf16[8,448,512]{2,1,0:T(8,128)(2,1)S(1)} %bitcast.68), channel_id=1, replica_groups=mesh['node'=8,'local'=4] {'node'}, dimensions={0} | all-to-all | bytes 7340032 | tf_op jit(solution)/shard_map/all_to_all | solution.py:26
  175.5 0.0 copy-start.5
  175.5 4.7 all-to-all-start.6
  180.2 0.0 copy-done.5
  180.2 4.7 gather_fusion.3
  184.9 4.7 gather_fusion.4
  189.5 6.9 broadcast_select_fusion
  196.4 64.8 %all-to-all-done.6 = bf16[8,64,3584]{2,1,0:T(8,128)(2,1)} async-done(((bf16[8,64,3584]{2,1,0:T(8,128)(2,1)}), bf16[8,64,3584]{2,1,0:T(8,128)(2,1)}, u32[]{:S(2)}, u32[]{:S(2)}) %all-to-all-start.6) | async-done | bytes 3670048 | tf_op jit(solution)/shard_map/all_to_all | solution.py:29
  261.2 86.0 %all_to_all.42 = bf16[8,448,512]{2,1,0:T(8,128)(2,1)} all-to-all(bf16[8,448,512]{2,1,0:T(8,128)(2,1)} %get-tuple-element.8), channel_id=1, replica_groups=mesh['node'=8,'local'=4] {'node'}, dimensions={0} | all-to-all | bytes 7340032 | tf_op jit(solution)/shard_map/all_to_all | solution.py:35
  347.3 0.0 copy-start.3
  347.3 0.0 copy-start.2
  347.3 4.6 all-to-all-start.5
  351.9 0.0 copy-done.3
  351.9 0.1 copy.21
  352.0 0.1 eq.45
  352.1 0.1 eq.38
  352.2 1.2 reduce-window.6
  353.4 0.2 slice_reduce_fusion
  353.6 0.0 copy-done.2
  353.7 0.0 copy-done.6
  353.7 0.1 select_reduce_fusion.1
  353.8 0.1 select_reduce_fusion
  353.9 2.4 scatter_custom_fusion
  356.4 5.4 gather_fusion
  361.8 71.0 %all-to-all-done.5 = bf16[8,448,512]{2,1,0:T(8,128)(2,1)} async-done(((bf16[8,448,512]{2,1,0:T(8,128)(2,1)}), bf16[8,448,512]{2,1,0:T(8,128)(2,1)}, u32[]{:S(2)}, u32[]{:S(2)}) %all-to-all-start.5) | async-done | bytes 3670048 | tf_op jit(solution)/shard_map/all_to_all | solution.py:36
  432.8 7.7 broadcast_in_dim.60
  440.5 3.7 all-to-all-start
  444.3 4.7 gather_fusion.2
  448.9 4.3 broadcast_select_fusion.2
  453.2 235.0 %all-to-all-done = bf16[32,48,3584]{2,1,0:T(8,128)(2,1)} async-done(((bf16[32,48,3584]{2,1,0:T(8,128)(2,1)}), bf16[32,48,3584]{2,1,0:T(8,128)(2,1)}, u32[]{:S(2)}, u32[]{:S(2)}) %all-to-all-start) | async-done | bytes 11010080 | tf_op jit(solution)/shard_map/all_to_all | solution.py:76
  688.2 4.5 all-to-all-start.7
  692.7 10.8 %fusion.4 = f32[1536,512]{1,0:T(8,128)} fusion(bf16[1536,3584]{1,0:T(8,128)(2,1)} %bitcast.5, bf16[1,3584,512]{2,1,0:T(8,128)(2,1)} %param.15), kind=kOutput, calls=%fused_computation.15 | convolution fusion | flops 5637144576 | bytes 17825792 | tf_op jit(solution)/shard_map/dot_general | solution.py:9
  703.6 19.4 %convolution_convert_fusion = bf16[1536,3584]{1,0:T(8,128)(2,1)} fusion(bf16[1,512,3584]{2,1,0:T(8,128)(2,1)} %param.17, bf16[1536,3584]{1,0:T(8,128)(2,1)} %bitcast.5, bf16[1,3584,512]{2,1,0:T(8,128)(2,1)} %param.16, f32[1536,512]{1,0:T(8,128)} %fusion.4), kind=kOutput, calls=%fused_computation.6 | convolution fusion | flops 11284512768 | bytes 32505856 | tf_op jit(solution)/shard_map/dot_general | solution.py:12
  723.0 51.8 %all-to-all-done.7 = bf16[8,64,3584]{2,1,0:T(8,128)(2,1)} async-done(((bf16[8,64,3584]{2,1,0:T(8,128)(2,1)}), bf16[8,64,3584]{2,1,0:T(8,128)(2,1)}, u32[]{:S(2)}, u32[]{:S(2)}) %all-to-all-start.7) | async-done | bytes 3670048 | tf_op jit(solution)/shard_map/all_to_all | solution.py:37
  774.8 4.0 all-to-all-start.1
  778.8 0.0 copy-done.4
  778.8 0.1 copy.26
  778.9 243.9 %all-to-all-done.1 = bf16[32,48,3584]{2,1,0:T(8,128)(2,1)} async-done(((bf16[32,48,3584]{2,1,0:T(8,128)(2,1)}), bf16[32,48,3584]{2,1,0:T(8,128)(2,1)}, u32[]{:S(2)}, u32[]{:S(2)}) %all-to-all-start.1) | async-done | bytes 11010080 | tf_op jit(solution)/shard_map/all_to_all | solution.py:78
  1022.8 8.2 add_convert_fusion
  1031.0 11.2 %gather_fusion.1 = bf16[512,3584]{1,0:T(8,128)(2,1)} fusion(bf16[768,3584]{1,0:T(8,128)(2,1)} %bitcast.61, s32[1024]{0:T(1024)S(1)} %pad_clamp_fusion.1), kind=kCustom, calls=%fused_computation.3 | custom fusion | bytes 7342080 | tf_op jit(solution)/shard_map/gather | solution.py:87
  1042.2 6.0 fusion
  1048.1 0.0 copy-done
  1048.1 1.8 copy.34
  1050.0 4.1 copy.35
  1054.1 4.1 copy.36
  (16 shorter events, 0.1 us)
Async XLA Ops:
  0.6 89.6 %copy-start.1 = (bf16[1,3584,512]{2,1,0:T(8,128)(2,1)S(1)}, bf16[1,3584,512]{2,1,0:T(8,128)(2,1)}, u32[]{:S(2)}) copy-start(bf16[1,3584,512]{2,1,0:T(8,128)(2,1)} %param.16) | copy-start | bytes 11010052
  175.5 4.7 copy-start.5
  175.5 85.7 %all-to-all-start.6 = ((bf16[8,64,3584]{2,1,0:T(8,128)(2,1)}), bf16[8,64,3584]{2,1,0:T(8,128)(2,1)}, u32[]{:S(2)}, u32[]{:S(2)}) async-start(bf16[8,64,3584]{2,1,0:T(8,128)(2,1)} %bitcast.67), calls=%async_computation.6 | async-start | bytes 7340032 | tf_op jit(solution)/shard_map/all_to_all | solution.py:29
  347.3 4.6 copy-start.3
  347.3 6.3 copy-start.2
  347.3 6.4 copy-start.6
  347.3 85.5 %all-to-all-start.5 = ((bf16[8,448,512]{2,1,0:T(8,128)(2,1)}), bf16[8,448,512]{2,1,0:T(8,128)(2,1)}, u32[]{:S(2)}, u32[]{:S(2)}) async-start(bf16[8,448,512]{2,1,0:T(8,128)(2,1)} %get-tuple-element.7), calls=%async_computation.5 | async-start | bytes 7340032 | tf_op jit(solution)/shard_map/all_to_all | solution.py:36
  440.5 247.7 %all-to-all-start = ((bf16[32,48,3584]{2,1,0:T(8,128)(2,1)}), bf16[32,48,3584]{2,1,0:T(8,128)(2,1)}, u32[]{:S(2)}, u32[]{:S(2)}) async-start(bf16[32,48,3584]{2,1,0:T(8,128)(2,1)} %bitcast.62), calls=%async_computation | async-start | bytes 22020096 | tf_op jit(solution)/shard_map/all_to_all | solution.py:76
  688.2 86.6 %all-to-all-start.7 = ((bf16[8,64,3584]{2,1,0:T(8,128)(2,1)}), bf16[8,64,3584]{2,1,0:T(8,128)(2,1)}, u32[]{:S(2)}, u32[]{:S(2)}) async-start(bf16[8,64,3584]{2,1,0:T(8,128)(2,1)} %broadcast_select_fusion.2), calls=%async_computation.7 | async-start | bytes 7340032 | tf_op jit(solution)/shard_map/all_to_all | solution.py:37
  774.7 4.0 copy-start.4
  774.8 248.1 %all-to-all-start.1 = ((bf16[32,48,3584]{2,1,0:T(8,128)(2,1)}), bf16[32,48,3584]{2,1,0:T(8,128)(2,1)}, u32[]{:S(2)}, u32[]{:S(2)}) async-start(bf16[32,48,3584]{2,1,0:T(8,128)(2,1)} %bitcast.65), calls=%async_computation.1 | async-start | bytes 22020096 | tf_op jit(solution)/shard_map/all_to_all | solution.py:78
  1042.2 6.0 copy-start
where the time goes:
time: 1060 us
  waiting for transfers between devices  666 us (63%)
  blocking collectives  261 us (25%)
  local copies, waits for them, and re-layouts  51.4 us (5%)
  matrix products  30.2 us (3%)
  other arithmetic  26.8 us (3%)
  starting transfers between devices  21.6 us (2%)
    all_to_all x1, waiting for transfers between devices, per_device(): lax.all_to_all(partial_value, ('node', 'local'), split_axis=0, concat_axi...  244 us
    all_to_all x1, waiting for transfers between devices, per_device(): lax.all_to_all(doubled, ('node', 'local'), split_axis=0, concat_axis=0, t...  235 us
    all_to_all x1, blocking collectives, move_weights(): lax.all_to_all(split_parts(gate_part, node_count), 'node', split_axis=0,...  89.6 us
    all_to_all x1, blocking collectives, move_weights(): lax.all_to_all(reordered[0], 'node', split_axis=0, concat_axis=0, tiled=T...  86 us
    all_to_all x1, blocking collectives, move_weights(): lax.all_to_all(split_parts(up_part, node_count), 'node', split_axis=0, co...  85.3 us
    all_to_all x1, waiting for transfers between devices, move_weights(): lax.all_to_all(reordered[1], 'node', split_axis=0, concat_axis=0, tiled=T...  71 us
    all_to_all x1, waiting for transfers between devices, move_weights(): lax.all_to_all(split_parts(down_part, node_count), 'node', split_axis=0,...  64.8 us
    all_to_all x1, waiting for transfers between devices, move_weights(): lax.all_to_all(reordered[2], 'node', split_axis=0, concat_axis=0, tiled=T...  51.8 us
  transfers between devices with their start and end apart: 5, of which 5 were waited for; matrix products, arithmetic and copies ran while one was open for 6% of the time, Pallas kernels for 0%

commit v1 on v0

v1 whole, which is shorter than its diff:
```python
import jax
import jax.numpy as jnp
import numpy as np
from jax import lax
from jax.sharding import PartitionSpec as P


def perfect_matchings(nodes):
    if not nodes:
        return [[]]
    first = nodes[0]
    found = []
    for other in nodes[1:]:
        rest = [n for n in nodes if n not in (first, other)]
        for tail in perfect_matchings(rest):
            found.append([(first, other)] + tail)
    return found


def matching_count(node_count):
    count = 1
    for odd in range(1, node_count, 2):
        count *= odd
    return count


def move_by_all_to_all(part, matching):
    node_count = lax.axis_size("node")
    pieces = part.reshape((node_count, part.shape[1] // node_count, part.shape[2]))
    arrived = lax.all_to_all(pieces, "node", split_axis=0, concat_axis=0, tiled=True)
    reordered = jnp.take(arrived, matching, axis=0)
    returned = lax.all_to_all(reordered, "node", split_axis=0, concat_axis=0, tiled=True)
    return returned.reshape(part.shape)


def matching_number(matching, table):
    same = jnp.all(jnp.asarray(table) == matching[None, :], axis=1)
    return jnp.sum(jnp.where(same, jnp.arange(table.shape[0], dtype=jnp.int32), 0))


def matching_table(node_count):
    couples = perfect_matchings(list(range(node_count)))
    table = np.zeros((len(couples), node_count), np.int32)
    for row, pairs in enumerate(couples):
        for a, b in pairs:
            table[row, a] = b
            table[row, b] = a
    return table


def move_weights(weights, matching):
    node_count = lax.axis_size("node")
    if matching_count(node_count) > 128:
        return tuple(move_by_all_to_all(part, matching) for part in weights)
    table = matching_table(node_count)

    def branch(row):
        pairs = [(int(table[row, n]), n) for n in range(node_count)]
        return lambda *parts: tuple(lax.ppermute(p, "node", pairs) for p in parts)

    branches = [branch(row) for row in range(table.shape[0])]
    return lax.switch(matching_number(matching, table), branches, *weights)


def per_device(
    tokens, expert_ids, gate_values, holder, matching, gate_weight, up_weight, down_weight
):
    gather_axes = ("local", "node")
    own = jnp.sum(
        jnp.where(expert_ids[:, :, None] == holder[None, None, :], gate_values[:, :, None], 0.0),
        axis=1,
    )
    all_gates = lax.all_gather(own, gather_axes, axis=0, tiled=True)
    rows = lax.all_gather(tokens, gather_axes, axis=0, tiled=True)
    (new_gate,) = move_weights((gate_weight,), matching)
    rows, new_gate = lax.optimization_barrier((rows, new_gate))
    slot = (lax.axis_index("node") * lax.axis_size("local") + lax.axis_index("local")) // 2
    share = lax.dynamic_slice_in_dim(all_gates, slot, 1, axis=1)
    gate_proj = jnp.dot(rows, gate_weight[0], preferred_element_type=jnp.float32)
    up_proj = jnp.dot(rows, up_weight[0], preferred_element_type=jnp.float32)
    hidden = (jax.nn.silu(gate_proj) * up_proj * share).astype(jnp.bfloat16)
    partial_value = jnp.dot(hidden, down_weight[0], preferred_element_type=jnp.float32)
    partial_value = partial_value.astype(jnp.bfloat16)
    partial_value, later_matching = lax.optimization_barrier((partial_value, matching))
    summed = lax.psum_scatter(partial_value, "local", scatter_dimension=0, tiled=True)
    combined = lax.psum_scatter(summed, "node", scatter_dimension=0, tiled=True)
    new_up, new_down = move_weights((up_weight, down_weight), later_matching)
    return (combined, new_gate, new_up, new_down)


def solution(mesh):
    in_specs = (
        P(("node", "local"), None),
        P(("node", "local"), None),
        P(("node", "local"), None),
        P(),
        P(),
        P(("node", "local"), None, None),
        P(("node", "local"), None, None),
        P(("node", "local"), None, None),
    )
    out_specs = (
        P(("node", "local"), None),
        P(("node", "local"), None, None),
        P(("node", "local"), None, None),
        P(("node", "local"), None, None),
    )
    return jax.shard_map(
        per_device, mesh=mesh, in_specs=in_specs, out_specs=out_specs, check_vma=False
    )
```

time: 1060 us -> 851 us (0.80); the launches traced: 1060 us -> 838 us
  blocking collectives: 261 us -> 73.5 us
  local copies, waits for them, and re-layouts: 51.4 us -> 12.6 us
  other arithmetic: 26.8 us -> 2.92 us
  waiting for transfers between devices: 666 us -> 683 us
  starting transfers between devices: 21.6 us -> 5.19 us
  between operations: 0.82 us -> 15.3 us
    all_to_all x5 -> x0, waiting for transfers between devices: 666 us -> none  [the longest x1 244 us: per_device(): lax.all_to_all(partial_value, ('node', 'local'), split_axis=0, concat_axi...]
    reduce_scatter x0 -> x2, waiting for transfers between devices: none -> 393 us  [the longest x1 202 us: per_device(): combined = lax.psum_scatter(summed, 'node', scatter_dimension=0, tiled=True)]
    ppermute x0 -> x3, waiting for transfers between devices: none -> 283 us  [branch(): return lambda *parts: tuple((lax.ppermute(p, 'node', pairs) for p in parts))]
    all_to_all x3 -> x0, blocking collectives: 261 us -> none  [the longest x1 89.6 us: move_weights(): lax.all_to_all(split_parts(gate_part, node_count), 'node', split_axis=0,...]
    all_gather x0 -> x1, blocking collectives: none -> 73.5 us  [per_device(): all_gates = lax.all_gather(own, gather_axes, axis=0, tiled=True)]
    gather x5 -> x0, local copies, waits for them, and re-layouts: 30.5 us -> none  [the longest x3 14 us: move_weights(): reordered = tuple((jnp.take(block, matching, axis=0) for block in arrived))]
    all_to_all x5 -> x0, starting transfers between devices: 21.6 us -> none  [the longest x1 4.66 us: move_weights(): lax.all_to_all(split_parts(down_part, node_count), 'node', split_axis=0,...]
    select_n x5 -> x0, other arithmetic: 11.2 us -> none  [the longest x3 11.2 us: move_weights(): reordered = tuple((jnp.take(block, matching, axis=0) for block in arrived))]
  transfers between devices with their start and end apart: 5 -> 6, of which waited for: 5 -> 6; matrix products, arithmetic and copies ran while one was open for 6% -> 0% of each run, Pallas kernels for 0% -> 0%
where the time goes in v1:
time: 851 us; the launch traced here: 838 us
  waiting for transfers between devices  683 us (80%)
  blocking collectives  73.5 us (9%)
  matrix products  38.1 us (4%)
  between operations  15.3 us (2%)
  local copies, waits for them, and re-layouts  12.6 us (1%)
    ppermute x3, waiting for transfers between devices, branch(): return lambda *parts: tuple((lax.ppermute(p, 'node', pairs) for p in parts))  283 us
    reduce_scatter x1, waiting for transfers between devices, per_device(): combined = lax.psum_scatter(summed, 'node', scatter_dimension=0, tiled=True)  202 us
    reduce_scatter x1, waiting for transfers between devices, per_device(): lax.psum_scatter(partial_value, 'local', scatter_dimension=0, tiled=True)  191 us
    all_gather x1, blocking collectives, per_device(): all_gates = lax.all_gather(own, gather_axes, axis=0, tiled=True)  73.5 us
    dot_general x1, matrix products, per_device(): jnp.dot(hidden, down_weight[0], preferred_element_type=jnp.float32)  24.7 us
  transfers between devices with their start and end apart: 6, of which 6 were waited for; matrix products, arithmetic and copies ran while one was open for 0% of the time, Pallas kernels for 0%

profile of v1, /device:TPU:0, one launch (start us, length us, event | category | flops | bytes accessed | tf_op | source)
XLA Modules:
  0.0 838.4 jit_solution(7095785496871817289)
XLA Ops:
  7.2 0.0 all-gather.3.cloned.1.call-start
  7.2 0.7 all-gather.3.cloned.1.call-update
  7.9 0.0 reduce-scatter.3.cloned.1.call-start
  8.0 0.8 select_reduce_fusion
  8.8 73.5 %all-gather = f32[32,64,16]{1,2,0:T(8,128)S(1)} all-gather(f32[1,64,16]{1,2,0:T(8,128)S(1)} %bitcast.19), channel_id=1, replica_groups=mesh['node'=8,'local'=4] {'local','node'}, dimensions={0}, use_global_device_ids=true | all-gather | bytes 135168 | tf_op jit(solution)/shard_map/all_gather | solution.py:73
  82.3 0.1 copy.23
  82.3 0.1 reshape.14
  82.5 0.8 compare_reduce_fusion.1
  83.2 0.6 select_reduce_fusion.2
  84.5 107.5 %conditional.2 = (bf16[1,3584,512]{2,1,0:T(8,128)(2,1)}) conditional(s32[]{:T(128)} %clamp.6, bf16[1,3584,512]{2,1,0:T(8,128)(2,1)} %param.225, bf16[1,3584,512]{2,1,0:T(8,128)(2,1)} %param.225, bf16[1,3584,512]{2,1,0:T(8,128)(2,1)} %param.225, bf16[1,3584,512]{2,1,0:T(8,128)(2,1)} %param.225, ...), branch_computations={%region_2.3_spmd, %region_3.4_spmd, %region_4.5_spmd, %region_5.6_... | conditional | bytes 14680112 | solution.py:62
  84.6 0.1 collective-permute-start.29
  84.6 107.1 %collective-permute-done.29 = bf16[1,3584,512]{2,1,0:T(8,128)(2,1)} collective-permute-done((bf16[1,3584,512]{2,1,0:T(8,128)(2,1)}, bf16[1,3584,512]{2,1,0:T(8,128)(2,1)}, u32[]{:S(2)}, u32[]{:S(2)}) %collective-permute-start.29) | collective-permute-done | bytes 3670048 | tf_op jit(solution)/shard_map/cond/branch_29_fun/ppermute | solution.py:59
  192.0 5.3 all-gather.3.cloned.1.call-done
  197.4 13.4 %fusion.1 = f32[2048,512]{1,0:T(8,128)} fusion(bf16[2048,3584]{1,0:T(8,128)(2,1)} %all-gather.3.cloned.1.call-done, bf16[1,3584,512]{2,1,0:T(8,128)(2,1)} %param.226), kind=kOutput, calls=%fused_computation.3 | convolution fusion | flops 7516192768 | bytes 22544384 | tf_op jit(solution)/shard_map/dot_general | solution.py:80
  210.7 24.7 %convolution_convert_fusion = bf16[2048,3584]{1,0:T(8,128)(2,1)} fusion(bf16[1,512,3584]{2,1,0:T(8,128)(2,1)} %param.227, f32[2048,512]{1,0:T(8,128)} %fusion.1, bf16[2048,3584]{1,0:T(8,128)(2,1)} %all-gather.3.cloned.1.call-done, bf16[1,3584,512]{2,1,0:T(8,128)(2,1)} %param.225, f32[2048]{0:T(1024)S(1)} %bitcast.20), kind=kOutput, calls=%fused_computation | convolution fusion | flops 15047065600 | bytes 40902656 | tf_op jit(solution)/shard_map/dot_general | solution.py:82
  235.4 0.0 reduce-scatter.3.cloned.1.call-update
  235.4 0.0 copy-start
  235.5 0.0 copy-start.1
  235.5 0.0 reduce-scatter.5.cloned.1.call-start
  235.5 191.0 %reduce-scatter.3.cloned.1.call-done = bf16[512,3584]{1,0:T(8,128)(2,1)} async-done(((bf16[2048,3584]{1,0:T(8,128)(2,1)}), bf16[512,3584]{1,0:T(8,128)(2,1)}) %reduce-scatter.3.cloned.1.call-update) | async-done | bytes 3670032 | tf_op jit(solution)/shard_map/reduce_scatter | solution.py:85
  426.5 0.0 reduce-scatter.5.cloned.1.call-update
  426.6 0.0 copy-done
  426.6 0.0 copy-done.1
  426.6 0.1 compare_reduce_fusion
  426.7 0.6 select_reduce_fusion.1
  428.0 189.0 %conditional.3 = (bf16[1,3584,512]{2,1,0:T(8,128)(2,1)}, bf16[1,512,3584]{2,1,0:T(8,128)(2,1)}) conditional(s32[]{:T(128)} %clamp.7, (bf16[1,3584,512]{2,1,0:T(8,128)(2,1)}, bf16[1,512,3584]{2,1,0:T(8,128)(2,1)}) %tuple.747, (bf16[1,3584,512]{2,1,0:T(8,128)(2,1)}, bf16[1,512,3584]{2,1,0:T(8,128)(2,1)}) %tuple.747, ...), branch_computations={%region_112.113_spmd, %region_113.114_spmd, %region_114.115_spmd, ... | conditional | bytes 29360224 | solution.py:62
  428.0 1.5 collective-permute-start.163
  429.5 3.5 collective-permute-start.164
  433.0 98.7 %collective-permute-done.163 = bf16[1,3584,512]{2,1,0:T(8,128)(2,1)} collective-permute-done((bf16[1,3584,512]{2,1,0:T(8,128)(2,1)}, bf16[1,3584,512]{2,1,0:T(8,128)(2,1)}, u32[]{:S(2)}, u32[]{:S(2)}) %collective-permute-start.163) | collective-permute-done | bytes 3670048 | tf_op jit(solution)/shard_map/cond/branch_29_fun/ppermute | solution.py:59
  531.7 77.5 %collective-permute-done.164 = bf16[1,512,3584]{2,1,0:T(8,128)(2,1)} collective-permute-done((bf16[1,512,3584]{2,1,0:T(8,128)(2,1)}, bf16[1,512,3584]{2,1,0:T(8,128)(2,1)}, u32[]{:S(2)}, u32[]{:S(2)}) %collective-permute-start.164) | collective-permute-done | bytes 3670048 | tf_op jit(solution)/shard_map/cond/branch_29_fun/ppermute | solution.py:59
  617.0 202.4 %reduce-scatter.5.cloned.1.call-done = bf16[64,3584]{1,0:T(8,128)(2,1)} async-done(((bf16[512,3584]{1,0:T(8,128)(2,1)}), bf16[64,3584]{1,0:T(8,128)(2,1)}) %reduce-scatter.5.cloned.1.call-update) | async-done | bytes 458768 | tf_op jit(solution)/shard_map/reduce_scatter | solution.py:86
  819.3 4.1 copy.342
  823.4 4.1 copy.343
  827.6 4.1 copy.344
  (1 shorter events, 0.0 us)
Async XLA Ops:
  7.2 190.2 %all-gather.3.cloned.1.call-start = ((), (), s32[]{:S(2)}) async-start(), calls=%async_computation.2 | async-start | bytes 15138816 | tf_op jit(solution)/shard_map/all_gather | solution.py:74
  7.9 418.6 %reduce-scatter.3.cloned.1.call-start = ((), (), s32[]{:S(2)}) async-start(), calls=%async_computation.3 | async-start | bytes 18350080 | tf_op jit(solution)/shard_map/reduce_scatter | solution.py:85
  84.6 107.2 %collective-permute-start.29 = (bf16[1,3584,512]{2,1,0:T(8,128)(2,1)}, bf16[1,3584,512]{2,1,0:T(8,128)(2,1)}, u32[]{:S(2)}, u32[]{:S(2)}) collective-permute-start(bf16[1,3584,512]{2,1,0:T(8,128)(2,1)} %param.29), channel_id=1, source_target_pairs={{8,0},{28,4},{0,8},{24,12},{20,16},{16,20},{12,24},{4,28},{9,1},{2... | collective-permute-start | bytes 11010056 | tf_op jit(solution)/shard_map/cond/branch_29_fun/ppermute | solution.py:59
  235.4 191.1 %copy-start = (s32[105,8]{0,1:T(8,128)S(1)}, s32[105,8]{0,1:T(8,128)}, u32[]{:S(2)}) copy-start(s32[105,8]{0,1:T(8,128)} %constant.39.clone) | copy-start | bytes 10084
  235.5 191.1 %copy-start.1 = (s32[8]{0:T(128)S(1)}, s32[8]{0:T(128)}, u32[]{:S(2)}) copy-start(s32[8]{0:T(128)} %param.224) | copy-start | bytes 100
  235.5 583.9 %reduce-scatter.5.cloned.1.call-start = ((), (), s32[]{:S(2)}) async-start(), calls=%async_computation.4 | async-start | bytes 4128768 | tf_op jit(solution)/shard_map/reduce_scatter | solution.py:86
  428.0 103.7 %collective-permute-start.163 = (bf16[1,3584,512]{2,1,0:T(8,128)(2,1)}, bf16[1,3584,512]{2,1,0:T(8,128)(2,1)}, u32[]{:S(2)}, u32[]{:S(2)}) collective-permute-start(bf16[1,3584,512]{2,1,0:T(8,128)(2,1)} %get-tuple-element.689), channel_id=1, source_target_pairs={{8,0},{28,4},{0,8},{24,12},{20,16},{16,20},{12,24},{4,28},{9,1},{2... | collective-permute-start | bytes 11010056 | tf_op jit(solution)/shard_map/cond/branch_29_fun/ppermute | solution.py:59
  429.5 179.7 %collective-permute-start.164 = (bf16[1,512,3584]{2,1,0:T(8,128)(2,1)}, bf16[1,512,3584]{2,1,0:T(8,128)(2,1)}, u32[]{:S(2)}, u32[]{:S(2)}) collective-permute-start(bf16[1,512,3584]{2,1,0:T(8,128)(2,1)} %get-tuple-element.690), channel_id=1, source_target_pairs={{8,0},{28,4},{0,8},{24,12},{20,16},{16,20},{12,24},{4,28},{9,1},{2... | collective-permute-start | bytes 11010056 | tf_op jit(solution)/shard_map/cond/branch_29_fun/ppermute | solution.py:59
Sparse Core Ops, SparseCore 0:
  10.8 186.4 all-gather.2
  235.6 190.9 reduce-scatter.2
  430.8 388.5 reduce-scatter.4
